TPU v7x, 512 devices: a whole 4x8x8 slice. The times are simulated.
512 devices in a mesh: leaf: 128 (over z, y, core), grp: 4 (over x).
Axes of the slice: x: 4, y: 8, z: 8, core: 2. Of those that a mesh axis runs over, the one named last changes fastest.
Arguments:
- points_in: bfloat16 [64, 262144], P('grp', 'leaf'), may hold values from -6 to 6
- leaf_basis: bfloat16 [32, 262144], P(None, 'leaf'), may hold values from -0.75 to 0.75
- transfer: bfloat16 [4096, 1024], P('leaf'), may hold values from -0.375 to 0.375
- far_blocks: bfloat16 [4096, 16, 1024], P('leaf'), may hold values from -0.25 to 0.25
- near_blocks: bfloat16 [4096, 8, 4096], P('leaf'), may hold values from -0.25 to 0.25
- near_leaf: int32 [4096, 8], P('leaf'), may hold values from 0 to 4095, as said below
- near_count: int32 [4096], P('leaf'), may hold values from 4 to 8, as said below
- far_slots: int32 [4096, 16], P('leaf'), may hold values from 0 to 127, as said below
- far_count: int32 [4096], P('leaf'), may hold values from 8 to 16, as said below
- recv_rows: int32 [128, 128, 1], P('leaf'), may hold values from 0 to 31
- coarse_blocks: bfloat16 [512, 16, 1024], P('leaf', 'grp'), may hold values from -0.25 to 0.25
- coarse_far: int32 [512, 16], P('leaf'), may hold values from 0 to 511, as said below
- coarse_count: int32 [512], P('leaf'), may hold values from 8 to 16, as said below
Outputs:
- field_out: bfloat16 [64, 262144], P('grp', 'leaf')
Inputs may be any that keep to these rules, and one draw needn't show every extreme that they name: near_leaf[l, 0] = l, and every entry lies within 4 leaves of l. `near_count`: some leaf has all 8 entries live. `far_slots`: entries index a device's requested slots flattened as owning device times 1 plus slot. `far_count`: some leaf has all 16 entries live. `coarse_far`: entries of coarse node c name coarse nodes held by the same aligned group of 16 indices of leaf as c. `coarse_count`: some coarse node has all 16 entries live.
All inputs are finite; a program needn't handle non-finite values.
Results may differ from a plain program's by a relative error of at most 0.0044.
Values may be sent and summed in bfloat16 or wider, within the bound.
A program may use at most 64 MiB of HBM per device.

v0:
```python
import jax
import jax.numpy as jnp
from jax import lax
from jax.sharding import PartitionSpec as P

PTS = 64
RANK = 32
CHILD = 8
WIN = 4


def swapped(value, axis, bit):
    mask = 2**bit
    pairs = [(source, source ^ mask) for source in range(lax.axis_size(axis))]
    return lax.ppermute(value, axis, pairs)


def with_halo(array, sides, width):
    for axis, dim in sides:
        count, length = (lax.axis_size(axis), array.shape[dim])
        up = [(i, (i + 1) % count) for i in range(count - 1)]
        down = [(j, i) for i, j in up]
        last = lax.slice_in_dim(array, length - width, length, axis=dim)
        initial = lax.slice_in_dim(array, 0, width, axis=dim)
        before = lax.ppermute(last, axis, up)
        after = lax.ppermute(initial, axis, down)
        array = jnp.concatenate([before, array, after], axis=dim)
    return array


def live_mask(counts, entries):
    return (
        lax.broadcasted_iota(jnp.int32, (counts.shape[0], entries), 1) < counts[:, None]
    ).astype(jnp.bfloat16)


def per_device(
    points_in,
    leaf_basis,
    transfer,
    far_blocks,
    near_blocks,
    near_leaf,
    near_count,
    far_slots,
    far_count,
    recv_rows,
    coarse_blocks,
    coarse_far,
    coarse_count,
):
    columns = points_in.shape[0]
    leaves = near_leaf.shape[0]
    far_entries = far_slots.shape[1]
    near_entries = near_leaf.shape[1]
    parents = coarse_far.shape[0]
    coarse_entries = coarse_far.shape[1]
    slot_count = recv_rows.shape[2]
    own_index = lax.axis_index("leaf")
    points_three = points_in.reshape(columns, leaves, PTS)
    basis_three = leaf_basis.reshape(RANK, leaves, PTS)
    coef = jnp.einsum(
        "rlp,qlp->lrq", basis_three, points_three, preferred_element_type=jnp.float32
    ).astype(jnp.bfloat16)
    coef_rows = coef.reshape(leaves, RANK * columns)
    maps = transfer.reshape(leaves, RANK, RANK)
    lifted = jnp.einsum("lrs,lsq->lrq", maps, coef, preferred_element_type=jnp.float32)
    parent = lifted.reshape(parents, CHILD, RANK, columns).sum(axis=1).astype(jnp.bfloat16)
    parent_rows = parent.reshape(parents, RANK * columns)
    group_size = min(16, lax.axis_size("leaf"))
    collected = parent_rows
    for level_bit in range(group_size.bit_length() - 1):
        partner = swapped(collected, "leaf", level_bit)
        upper_half = own_index >> level_bit & 1 == 1
        collected = jnp.where(
            upper_half,
            jnp.concatenate([partner, collected], axis=0),
            jnp.concatenate([collected, partner], axis=0),
        )
    group_start = own_index // group_size * group_size * parents
    coarse_source = collected[coarse_far - group_start]
    couplings = lax.all_gather(coarse_blocks, "grp", axis=1, tiled=True)
    coarse_mask = live_mask(coarse_count, coarse_entries)
    coarse_weights = (
        couplings.reshape(parents, coarse_entries, RANK, RANK) * coarse_mask[:, :, None, None]
    )
    coarse_source = coarse_source.reshape(parents, coarse_entries, RANK, columns)
    coarse_field = jnp.einsum(
        "ckrs,cksq->crq", coarse_weights, coarse_source, preferred_element_type=jnp.float32
    ).astype(jnp.bfloat16)
    down = jnp.einsum(
        "lrs,lrq->lsq",
        maps,
        jnp.repeat(coarse_field, CHILD, axis=0),
        preferred_element_type=jnp.float32,
    )
    every_leaf = lax.all_gather(coef_rows, "leaf", axis=0, tiled=True)
    table = recv_rows[0].reshape(-1)
    source = far_slots // slot_count * leaves + table[far_slots]
    far_source = every_leaf[source]
    far_mask = live_mask(far_count, far_entries)
    far_weights = far_blocks.reshape(leaves, far_entries, RANK, RANK) * far_mask[:, :, None, None]
    far_part = jnp.einsum(
        "lkrs,lksq->lrq",
        far_weights,
        far_source.reshape(leaves, far_entries, RANK, columns),
        preferred_element_type=jnp.float32,
    )
    local = (far_part + down).astype(jnp.bfloat16)
    padded = with_halo(points_in, (("leaf", 1),), WIN * PTS)
    padded_three = padded.reshape(columns, leaves + 2 * WIN, PTS)
    positions = near_leaf - own_index * leaves + WIN
    near_source = padded_three[:, positions]
    near_mask = live_mask(near_count, near_entries)
    near_weights = near_blocks.reshape(leaves, near_entries, PTS, PTS) * near_mask[:, :, None, None]
    near = jnp.einsum(
        "lkps,qlks->qlp", near_weights, near_source, preferred_element_type=jnp.float32
    )
    result = (
        jnp.einsum("rlp,lrq->qlp", basis_three, local, preferred_element_type=jnp.float32) + near
    )
    return result.reshape(columns, leaves * PTS).astype(jnp.bfloat16)


def solution(mesh):
    in_specs = (
        P("grp", "leaf"),
        P(None, "leaf"),
        P("leaf", None),
        P("leaf", None, None),
        P("leaf", None, None),
        P("leaf", None),
        P("leaf"),
        P("leaf", None),
        P("leaf"),
        P("leaf", None, None),
        P("leaf", "grp", None),
        P("leaf", None),
        P("leaf"),
    )
    out_specs = P("grp", "leaf")
    return jax.shard_map(
        per_device, mesh=mesh, in_specs=in_specs, out_specs=out_specs, check_vma=False
    )
```

profile of v0, /device:TPU:1, one launch (start us, length us, event | category | flops | bytes accessed | tf_op | source)
XLA Modules:
  0.0 123.8 jit_solution(17531624199770484824)
XLA Ops:
  6.5 1.2 reshape.102
  7.7 1.0 reshape.103
  8.8 0.2 convolution_convert_fusion
  9.0 0.2 copy.49
  9.2 0.7 copy.50
  9.9 0.0 all-gather.2.cloned.1.call-update
  10.0 0.7 fusion.24
  10.7 8.8 %collective-permute-start.5 = (bf16[16,256]{1,0:T(8,128)(2,1)S(1)}, bf16[16,256]{1,0:T(8,128)(2,1)S(1)}, u32[]{:S(2)}, u32[]{:S(2)}) collective-permute-start(bf16[16,256]{1,0:T(8,128)(2,1)S(1)} %get-tuple-element.6), channel_id=1, source_target_pairs={{4,0},{8,4},{12,8},{16,12},{20,16},{24,20},{28,24},{32,28},{36,32}... | collective-permute-start | bytes 24584 | tf_op jit(solution)/shard_map/ppermute | solution.py:26
  19.5 1.9 %collective-permute-start.4 = (bf16[16,256]{1,0:T(8,128)(2,1)S(1)}, bf16[16,256]{1,0:T(8,128)(2,1)S(1)}, u32[]{:S(2)}, u32[]{:S(2)}) collective-permute-start(bf16[16,256]{1,0:T(8,128)(2,1)S(1)} %get-tuple-element.5), channel_id=1, source_target_pairs={{0,4},{4,8},{8,12},{12,16},{16,20},{20,24},{24,28},{28,32},{32,36}... | collective-permute-start | bytes 24584 | tf_op jit(solution)/shard_map/ppermute | solution.py:25
  21.4 1.1 reshape.107
  22.5 0.2 bitcast_reduce_fusion
  22.7 0.1 copy.58
  22.8 0.1 convert_element_type.50
  22.9 2.4 %collective-permute-start = (bf16[4,512]{1,0:T(4,128)(2,1)S(1)}, bf16[4,512]{1,0:T(4,128)(2,1)S(1)}, u32[]{:S(2)}, u32[]{:S(2)}) collective-permute-start(bf16[4,512]{1,0:T(4,128)(2,1)S(1)} %convert_element_type.50), channel_id=1, source_target_pairs={{0,4},{4,0},{8,12},{12,8},{16,20},{20,16},{24,28},{28,24},{32,36},... | collective-permute-start | bytes 12296 | tf_op jit(solution)/shard_map/ppermute | solution.py:15
  25.4 0.7 compare_select_fusion.2
  26.0 0.1 copy.61
  26.1 0.1 reshape.139
  26.2 0.8 copy.51
  27.0 0.1 reshape.115
  27.1 0.0 copy-start.4
  27.2 3.3 %gather_fusion = s32[512]{0:T(512)S(1)} fusion(s32[128]{0:T(128)S(1)} %bitcast.40, s32[1024]{0:T(1024)S(1)} %pad_clamp_fusion.3), kind=kCustom, calls=%fused_computation | custom fusion | bytes 6144 | tf_op jit(solution)/shard_map/gather | solution.py:99
  30.5 0.1 reshape.114
  30.6 0.1 reshape.123
  30.7 0.1 reshape.131
  30.8 0.1 fusion.23
  30.9 0.1 fusion.22
  31.0 0.1 fusion.21
  31.1 1.9 %collective-permute-start.1 = (bf16[8,512]{1,0:T(8,128)(2,1)S(1)}, bf16[8,512]{1,0:T(8,128)(2,1)S(1)}, u32[]{:S(2)}, u32[]{:S(2)}) collective-permute-start(bf16[8,512]{1,0:T(8,128)(2,1)S(1)} %maximum_select_fusion.3), channel_id=1, source_target_pairs={{0,8},{4,12},{8,0},{12,4},{16,24},{20,28},{24,16},{28,20},{32,40},... | collective-permute-start | bytes 24584 | tf_op jit(solution)/shard_map/ppermute | solution.py:15
  33.1 9.6 %all_gather.7 = bf16[4,16,1024]{2,0,1:T(4,128)(2,1)S(1)} all-gather(bf16[4,4,1024]{2,0,1:T(4,128)(2,1)S(1)} %copy.56), channel_id=1, replica_groups=mesh['leaf'=128,'grp'=4] {'grp'}, dimensions={1}, use_global_device_ids=true | all-gather | bytes 163840 | tf_op jit(solution)/shard_map/all_gather | solution.py:82
  42.7 5.5 %reshape.112 = bf16[32,8,64,64]{3,2,1,0:T(8,128)(2,1)} reshape(bf16[32,8,4096]{2,1,0:T(8,128)(2,1)S(1)} %copy-done.1) | data formatting | bytes 4194304 | tf_op jit(solution)/shard_map/reshape | solution.py:115
  48.2 6.3 %reshape.101 = bf16[32,16,32,32]{3,2,1,0:T(8,128)(2,1)} reshape(bf16[32,16,1024]{2,1,0:T(8,128)(2,1)} %param.16) | data formatting | bytes 2097152 | tf_op jit(solution)/shard_map/reshape | solution.py:102
  54.5 0.3 reshape.106
  54.8 2.6 %collective-permute-start.2 = (bf16[16,512]{1,0:T(8,128)(2,1)S(1)}, bf16[16,512]{1,0:T(8,128)(2,1)S(1)}, u32[]{:S(2)}, u32[]{:S(2)}) collective-permute-start(bf16[16,512]{1,0:T(8,128)(2,1)S(1)} %maximum_select_fusion.2), channel_id=1, source_target_pairs={{0,16},{4,20},{8,24},{12,28},{16,0},{20,4},{24,8},{28,12},{32,48},... | collective-permute-start | bytes 49160 | tf_op jit(solution)/shard_map/ppermute | solution.py:15
  57.5 0.2 reshape.111
  57.7 0.8 gather_fusion.3
  58.5 1.7 %collective-permute-done.2 = bf16[16,512]{1,0:T(8,128)(2,1)S(1)} collective-permute-done((bf16[16,512]{1,0:T(8,128)(2,1)S(1)}, bf16[16,512]{1,0:T(8,128)(2,1)S(1)}, u32[]{:S(2)}, u32[]{:S(2)}) %collective-permute-start.2) | collective-permute-done | bytes 16416 | tf_op jit(solution)/shard_map/ppermute | solution.py:15
  60.2 3.9 %collective-permute-start.3 = (bf16[32,512]{1,0:T(8,128)(2,1)S(1)}, bf16[32,512]{1,0:T(8,128)(2,1)S(1)}, u32[]{:S(2)}, u32[]{:S(2)}) collective-permute-start(bf16[32,512]{1,0:T(8,128)(2,1)S(1)} %maximum_select_fusion.1), channel_id=1, source_target_pairs={{0,32},{4,36},{8,40},{12,44},{16,48},{20,52},{24,56},{28,60},{32,0... | collective-permute-start | bytes 98312 | tf_op jit(solution)/shard_map/ppermute | solution.py:15
  64.1 3.5 %fusion.6 = f32[32,16,64]{2,1,0:T(8,128)S(1)} fusion(bf16[16,32,8,64]{3,0,2,1:T(8,128)(2,1)S(1)} %bitcast.41, bf16[32,8,64,64]{3,2,1,0:T(8,128)(2,1)} %reshape.112, bf16[32,8]{1,0:T(8,128)(2,1)S(1)} %fusion.22), kind=kOutput, calls=%fused_computation.10 | convolution fusion | flops 34603008 | bytes 2753024 | tf_op jit(solution)/shard_map/lkps,qlks->qlp/dot_general | solution.py:116
  67.5 1.2 %collective-permute-done.3 = bf16[32,512]{1,0:T(8,128)(2,1)S(1)} collective-permute-done((bf16[32,512]{1,0:T(8,128)(2,1)S(1)}, bf16[32,512]{1,0:T(8,128)(2,1)S(1)}, u32[]{:S(2)}, u32[]{:S(2)}) %collective-permute-start.3) | collective-permute-done | bytes 32800 | tf_op jit(solution)/shard_map/ppermute | solution.py:15
  68.8 0.7 gather_fusion.2
  69.5 0.4 reshape.109
  69.9 0.4 fusion.16
  70.3 30.8 %all-gather.2.cloned.1.call-done = bf16[4096,512]{1,0:T(8,128)(2,1)} async-done(((bf16[32,512]{1,0:T(8,128)(2,1)}), bf16[4096,512]{1,0:T(8,128)(2,1)}) %all-gather.2.cloned.1.call-update) | async-done | bytes 4194320 | tf_op jit(solution)/shard_map/all_gather | solution.py:97
  101.2 4.7 %gather_fusion.1 = bf16[512,512]{1,0:T(8,128)(2,1)S(1)} fusion(bf16[4096,512]{1,0:T(8,128)(2,1)} %all-gather.2.cloned.1.call-done, s32[1024]{0:T(1024)S(1)} %pad_clamp_fusion.2), kind=kCustom, calls=%fused_computation.1 | custom fusion | bytes 1050624 | tf_op jit(solution)/shard_map/gather | solution.py:100
  105.9 4.5 %reshape.105 = bf16[32,16,32,16]{3,2,1,0:T(8,128)(2,1)} reshape(bf16[512,512]{1,0:T(8,128)(2,1)S(1)} %gather_fusion.1) | data formatting | bytes 1048576 | tf_op jit(solution)/shard_map/reshape | solution.py:106
  110.4 5.3 %fusion.10 = f32[32,32,16]{1,2,0:T(8,128)S(1)} fusion(bf16[32,16,32,16]{3,2,1,0:T(8,128)(2,1)} %reshape.105, bf16[32,16,32,32]{3,2,1,0:T(8,128)(2,1)} %reshape.101, bf16[32,16]{1,0:T(8,128)(2,1)S(1)} %fusion.21), kind=kOutput, calls=%fused_computation.14 | convolution fusion | flops 17301504 | bytes 1639424 | tf_op jit(solution)/shard_map/lkrs,lksq->lrq/dot_general | solution.py:103
  115.7 0.3 fusion.15
  116.1 0.8 convert_element_type.56
  (36 shorter events, 0.3 us)
Async XLA Ops:
  6.5 20.6 %copy-start = (s32[1,128,1]{1,2,0:T(1,128)S(1)}, s32[1,128,1]{1,2,0:T(1,128)}, u32[]{:S(2)}) copy-start(s32[1,128,1]{1,2,0:T(1,128)} %param.22) | copy-start | bytes 1540
  6.5 94.6 %all-gather.2.cloned.1.call-start = ((), (), s32[]{:S(2)}) async-start(), calls=%async_computation | async-start | bytes 4227072 | tf_op jit(solution)/shard_map/all_gather | solution.py:97
  10.7 46.7 %collective-permute-start.5 = (bf16[16,256]{1,0:T(8,128)(2,1)S(1)}, bf16[16,256]{1,0:T(8,128)(2,1)S(1)}, u32[]{:S(2)}, u32[]{:S(2)}) collective-permute-start(bf16[16,256]{1,0:T(8,128)(2,1)S(1)} %get-tuple-element.6), channel_id=1, source_target_pairs={{4,0},{8,4},{12,8},{16,12},{20,16},{24,20},{28,24},{32,28},{36,32}... | collective-permute-start | bytes 24584 | tf_op jit(solution)/shard_map/ppermute | solution.py:26
  19.5 38.0 %collective-permute-start.4 = (bf16[16,256]{1,0:T(8,128)(2,1)S(1)}, bf16[16,256]{1,0:T(8,128)(2,1)S(1)}, u32[]{:S(2)}, u32[]{:S(2)}) collective-permute-start(bf16[16,256]{1,0:T(8,128)(2,1)S(1)} %get-tuple-element.5), channel_id=1, source_target_pairs={{0,4},{4,8},{8,12},{12,16},{16,20},{20,24},{24,28},{28,32},{32,36}... | collective-permute-start | bytes 24584 | tf_op jit(solution)/shard_map/ppermute | solution.py:25
  22.9 8.2 %collective-permute-start = (bf16[4,512]{1,0:T(4,128)(2,1)S(1)}, bf16[4,512]{1,0:T(4,128)(2,1)S(1)}, u32[]{:S(2)}, u32[]{:S(2)}) collective-permute-start(bf16[4,512]{1,0:T(4,128)(2,1)S(1)} %convert_element_type.50), channel_id=1, source_target_pairs={{0,4},{4,0},{8,12},{12,8},{16,20},{20,16},{24,28},{28,24},{32,36},... | collective-permute-start | bytes 12296 | tf_op jit(solution)/shard_map/ppermute | solution.py:15
  27.1 3.6 %copy-start.4 = (s32[4,16]{1,0:T(4,128)S(1)}, s32[4,16]{1,0:T(4,128)}, u32[]{:S(2)}) copy-start(s32[4,16]{1,0:T(4,128)} %param.24) | copy-start | bytes 772
  27.1 3.7 %copy-start.7 = (s32[4]{0:T(128)S(1)}, s32[4]{0:T(128)}, u32[]{:S(2)}) copy-start(s32[4]{0:T(128)} %param.25) | copy-start | bytes 52
  27.1 3.8 %copy-start.5 = (s32[32]{0:T(128)S(1)}, s32[32]{0:T(128)}, u32[]{:S(2)}) copy-start(s32[32]{0:T(128)} %param.19) | copy-start | bytes 388
  27.1 3.8 %copy-start.6 = (s32[32]{0:T(128)S(1)}, s32[32]{0:T(128)}, u32[]{:S(2)}) copy-start(s32[32]{0:T(128)} %param.21) | copy-start | bytes 388
  27.1 3.9 %copy-start.3 = (bf16[4,4,1024]{2,1,0:T(4,128)(2,1)S(1)}, bf16[4,4,1024]{2,1,0:T(4,128)(2,1)}, u32[]{:S(2)}) copy-start(bf16[4,4,1024]{2,1,0:T(4,128)(2,1)} %param.23) | copy-start | bytes 98308
  27.2 15.5 %copy-start.1 = (bf16[32,8,4096]{2,1,0:T(8,128)(2,1)S(1)}, bf16[32,8,4096]{2,1,0:T(8,128)(2,1)}, u32[]{:S(2)}) copy-start(bf16[32,8,4096]{2,1,0:T(8,128)(2,1)} %param.17) | copy-start | bytes 6291460
  31.1 23.7 %collective-permute-start.1 = (bf16[8,512]{1,0:T(8,128)(2,1)S(1)}, bf16[8,512]{1,0:T(8,128)(2,1)S(1)}, u32[]{:S(2)}, u32[]{:S(2)}) collective-permute-start(bf16[8,512]{1,0:T(8,128)(2,1)S(1)} %maximum_select_fusion.3), channel_id=1, source_target_pairs={{0,8},{4,12},{8,0},{12,4},{16,24},{20,28},{24,16},{28,20},{32,40},... | collective-permute-start | bytes 24584 | tf_op jit(solution)/shard_map/ppermute | solution.py:15
  48.2 9.3 %copy-start.2 = (bf16[16,2048]{1,0:T(8,128)(2,1)S(1)}, bf16[16,2048]{1,0:T(8,128)(2,1)}, u32[]{:S(2)}) copy-start(bf16[16,2048]{1,0:T(8,128)(2,1)} %param.13) | copy-start | bytes 196612
  54.8 5.4 %collective-permute-start.2 = (bf16[16,512]{1,0:T(8,128)(2,1)S(1)}, bf16[16,512]{1,0:T(8,128)(2,1)S(1)}, u32[]{:S(2)}, u32[]{:S(2)}) collective-permute-start(bf16[16,512]{1,0:T(8,128)(2,1)S(1)} %maximum_select_fusion.2), channel_id=1, source_target_pairs={{0,16},{4,20},{8,24},{12,28},{16,0},{20,4},{24,8},{28,12},{32,48},... | collective-permute-start | bytes 49160 | tf_op jit(solution)/shard_map/ppermute | solution.py:15
  60.2 8.6 %collective-permute-start.3 = (bf16[32,512]{1,0:T(8,128)(2,1)S(1)}, bf16[32,512]{1,0:T(8,128)(2,1)S(1)}, u32[]{:S(2)}, u32[]{:S(2)}) collective-permute-start(bf16[32,512]{1,0:T(8,128)(2,1)S(1)} %maximum_select_fusion.1), channel_id=1, source_target_pairs={{0,32},{4,36},{8,40},{12,44},{16,48},{20,52},{24,56},{28,60},{32,0... | collective-permute-start | bytes 98312 | tf_op jit(solution)/shard_map/ppermute | solution.py:15
Sparse Core Ops, SparseCore 0:
  10.5 90.6 all-gather.1
where the time goes:
time: 124 us
  local copies, waits for them, and re-layouts  34.1 us (28%)
  waiting for transfers between devices  33.8 us (27%)
  starting transfers between devices  21.5 us (17%)
  between operations  13.7 us (11%)
  matrix products  9.99 us (8%)
  blocking collectives  9.6 us (8%)
    all_gather x1, waiting for transfers between devices, per_device(): every_leaf = lax.all_gather(coef_rows, 'leaf', axis=0, tiled=True)  30.8 us
    ppermute x4, starting transfers between devices, swapped(): return lax.ppermute(value, axis, pairs)  10.8 us
    all_gather x1, blocking collectives, per_device(): couplings = lax.all_gather(coarse_blocks, 'grp', axis=1, tiled=True)  9.6 us
    ppermute x1, starting transfers between devices, with_halo(): after = lax.ppermute(initial, axis, down)  8.77 us
    reshape x1, local copies, waits for them, and re-layouts, per_device(): far_blocks.reshape(leaves, far_entries, RANK, RANK)  6.31 us
    reshape x1, local copies, waits for them, and re-layouts, per_device(): near_blocks.reshape(leaves, near_entries, PTS, PTS)  5.54 us
    dot_general x1, matrix products, per_device(): jnp.einsum('lkrs,lksq->lrq', far_weights, far_source.reshape(leaves, far_...  5.32 us
    gather x1, local copies, waits for them, and re-layouts, per_device(): far_source = every_leaf[source]  4.71 us
  transfers between devices with their start and end apart: 7, of which 3 were waited for; matrix products, arithmetic and copies ran while one was open for 21% of the time, Pallas kernels for 0%

commit v1 on v0

v1 whole, which is shorter than its diff:
```python
import jax
import jax.numpy as jnp
from jax import lax
from jax.experimental import pallas as pl
from jax.experimental.pallas import tpu as pltpu
from jax.sharding import PartitionSpec as P

BF = jnp.bfloat16
F32 = jnp.float32
MESH = pl.DeviceIdType.MESH


def dot_nt(a, b):
    return lax.dot_general(a, b, (((1,), (1,)), ((), ())), preferred_element_type=F32)


def dot_nn(a, b):
    return jnp.dot(a, b, preferred_element_type=F32)


def iotas(shape):
    row = lax.broadcasted_iota(jnp.int32, shape, 0)
    col = lax.broadcasted_iota(jnp.int32, shape, 1)
    return row, col


def ones_where(cond):
    return jnp.where(cond, 1.0, 0.0).astype(BF)


def expand(tiles):
    _, col = iotas((8, 128))
    masks = [jnp.where((col >> 5) == r4, 1.0, 0.0) for r4 in range(4)]
    return jnp.concatenate([tile * mask for tile in tiles for mask in masks], axis=0).astype(BF)


def lane_tiles(value):
    return [value[:, 128 * t : 128 * t + 128] for t in range(value.shape[1] // 128)]


def diagonal(product, rows, entries):
    _, col = iotas((rows, product.shape[1]))
    kept = product[0:rows]
    for k in range(1, entries):
        kept = jnp.where((col & (entries - 1)) == k, product[rows * k : rows * k + rows], kept)
    return kept


def spread_matrix():
    row, col = iotas((128, 512))
    return ones_where(((row >> 5) == (col >> 7)) & ((row & 31) == (col & 31)))


def place_matrix(j):
    row, col = iotas((128, 512))
    return ones_where(((row >> 5) == (col >> 7)) & ((col & 127) == (j * 32 + (row & 31))))


def kernel(
    points_h,
    basis_h,
    transfer_h,
    far_h,
    near_h,
    near_leaf_h,
    near_count_h,
    far_slots_h,
    far_count_h,
    recv_h,
    coarse_h,
    coarse_far_h,
    coarse_count_h,
    out_ref,
    pts,
    bas,
    trn,
    farv,
    nearv,
    cb,
    halo,
    p1,
    rown,
    pw,
    tp,
    r2,
    send,
    fbuf,
    tt,
    bx,
    tn,
    nr,
    nf,
    fr,
    dr,
    idxv,
    idxs,
    nls,
    ncs,
    fss,
    fcs,
    cfs,
    ccs,
    load_sem,
    idx_ssem,
    idx_rsem,
    p1_ssem,
    p1_rsem,
    p2_ssem,
    p2_rsem,
    pw_ssem,
    pw_rsem,
    halo_ssem,
    halo_rsem,
    cb_ssem,
    cb_rsem,
):
    me = lax.axis_index("leaf")
    grp = lax.axis_index("grp")
    core = lax.rem(me, 2)
    ylo = lax.rem(lax.div(me, 2), 2)
    yhi = lax.rem(lax.div(me, 4), 4)
    zlo = lax.rem(lax.div(me, 16), 2)
    zhi = lax.div(me, 32)
    member = zlo * 4 + ylo * 2 + core
    in_group = lax.rem(me, 16)

    def cube_peer(o):
        c = lax.rem(core + (o & 1), 2)
        y = lax.rem(ylo + ((o >> 1) & 1), 2)
        z = lax.rem(zlo + ((o >> 2) & 1), 2)
        return (zhi * 32 + z * 16 + yhi * 4 + y * 2 + c, grp)

    def far_peer(o):
        z = lax.rem(zhi + (o >> 2), 4)
        y = lax.rem(yhi + (o & 3), 4)
        return (z * 32 + zlo * 16 + y * 4 + ylo * 2 + core, grp)

    def group_peer(o):
        return (lax.div(me, 16) * 16 + lax.rem(in_group + o, 16), grp)

    up = (lax.rem(me + 1, 128), grp)
    down = (lax.rem(me + 127, 128), grp)

    def grp_peer(o):
        return (me, lax.rem(grp + o, 4))

    loads = {}

    def load(name, src, dst, n):
        loads[name] = pltpu.make_async_copy(src, dst, load_sem.at[n])
        loads[name].start()

    load("points", points_h, pts, 0)
    load("basis", basis_h, bas, 1)
    load("transfer", transfer_h, trn, 2)
    load("recv", recv_h, idxv.at[0], 3)
    load("coarse", coarse_h, cb.at[grp], 4)

    barrier = pltpu.get_barrier_semaphore()
    peers = [cube_peer(o) for o in range(1, 8)]
    peers += [far_peer(o) for o in range(1, 16)]
    peers += [group_peer(o) for o in range(1, 16)]
    peers += [up, down]
    peers += [grp_peer(o) for o in range(1, 4)]
    for peer in peers:
        pl.semaphore_signal(barrier, inc=1, device_id=peer, device_id_type=MESH)

    load("near_leaf", near_leaf_h, nls, 5)
    load("near_count", near_count_h, ncs, 6)
    load("far_slots", far_slots_h, fss, 7)
    load("far_count", far_count_h, fcs, 8)
    load("coarse_far", coarse_far_h, cfs, 9)
    load("coarse_count", coarse_count_h, ccs, 10)
    load("near", near_h, nearv, 11)
    load("far", far_h, farv, 12)

    loads["points"].wait()
    loads["basis"].wait()
    _, col = iotas((32, 256))
    quad_masks = [ones_where((col >> 6) == l4) for l4 in range(4)]
    for quad in range(8):
        lanes = slice(256 * quad, 256 * quad + 256)
        v = bas[:, lanes]
        vv = jnp.concatenate([v * mask for mask in quad_masks], axis=0)
        p1[member, quad] = dot_nt(pts[:, lanes], vv).astype(BF)

    spread = spread_matrix()
    wide = dot_nn(p1[member].reshape(128, 128), spread).astype(BF)
    for quad in range(8):
        for a in range(4):
            rown[4 * quad + a] = wide[16 * quad : 16 * quad + 16, 128 * a : 128 * a + 128]
    loads["transfer"].wait()
    total = jnp.zeros((16, 128), F32)
    row, col = iotas((256, 128))
    for c in range(4):
        ex = expand(lane_tiles(trn[8 * c : 8 * c + 8, :].astype(F32)))
        product = dot_nt(rown[8 * c : 8 * c + 8].reshape(128, 128), ex)
        kept = diagonal(product, 16, 8).astype(BF)
        total += dot_nn(kept, ones_where(col == c * 32 + (row >> 3)))
    pw[in_group] = total.astype(BF)

    loads["recv"].wait()
    loads["coarse"].wait()
    pl.semaphore_wait(barrier, len(peers))

    sends = []

    def remote(src, dst, ssem, rsem, peer):
        copy = pltpu.make_async_remote_copy(
            src_ref=src,
            dst_ref=dst,
            send_sem=ssem,
            recv_sem=rsem,
            device_id=peer,
            device_id_type=MESH,
        )
        copy.start()
        sends.append(copy)
        return copy

    p1_copies = [
        remote(p1.at[member], p1.at[member], p1_ssem.at[o], p1_rsem.at[o], cube_peer(o))
        for o in range(1, 8)
    ]
    idx_copies = [
        remote(idxv.at[0], idxv.at[o], idx_ssem.at[o], idx_rsem.at[o], far_peer(o))
        for o in range(1, 16)
    ]
    halo_copies = [
        remote(pts.at[:, pl.ds(1792, 256)], halo.at[0], halo_ssem.at[0], halo_rsem.at[0], up),
        remote(pts.at[:, pl.ds(0, 256)], halo.at[1], halo_ssem.at[1], halo_rsem.at[1], down),
    ]
    pw_copies = [
        remote(pw.at[in_group], pw.at[in_group], pw_ssem.at[o], pw_rsem.at[o], group_peer(o))
        for o in range(1, 16)
    ]
    cb_copies = [
        remote(cb.at[grp], cb.at[grp], cb_ssem.at[o], cb_rsem.at[o], grp_peer(o))
        for o in range(1, 4)
    ]

    loads["far"].wait()
    loads["far_count"].wait()

    def prepare(l, _):
        count = fcs[0, l]
        sub, _ = iotas((8, 128))
        low = jnp.where(sub < count, 1.0, 0.0)
        high = jnp.where(sub + 8 < count, 1.0, 0.0)
        blocks = farv[l].astype(F32)
        bx[l, :, 0:128] = expand([tile * low for tile in lane_tiles(blocks[0:8])])
        bx[l, :, 128:256] = expand([tile * high for tile in lane_tiles(blocks[8:16])])
        return 0

    lax.fori_loop(0, 32, prepare, 0)

    _, col = iotas((16, 128))
    left = jnp.where(col < 64, 1.0, 0.0)
    right = 1.0 - left

    def near_table(m, tile):
        value = tile.astype(F32)
        turned = pltpu.roll(value, 64, 1)
        tn[m] = jnp.concatenate([value * left, turned * right], axis=0).astype(BF)
        tn[m + 1] = jnp.concatenate([turned * left, value * right], axis=0).astype(BF)

    for j in range(16):
        near_table(4 + 2 * j, pts[:, 128 * j : 128 * j + 128])
    for copy in halo_copies:
        copy.wait_recv()
    for j in range(2):
        near_table(2 * j, halo[0, :, 128 * j : 128 * j + 128])
        near_table(36 + 2 * j, halo[1, :, 128 * j : 128 * j + 128])
    loads["near"].wait()
    loads["near_leaf"].wait()
    loads["near_count"].wait()

    def near_pair(j, _):
        _, lane = iotas((32, 256))
        for l2 in range(2):
            l = 2 * j + l2
            blocks = nearv[l].astype(F32)
            flat = jnp.concatenate(lane_tiles(blocks), axis=0).astype(BF)
            source = jnp.concatenate(
                [tn[jnp.clip(nls[k, l] - me * 32 + 4, 0, 39)] for k in range(8)], axis=0
            )
            kept = diagonal(dot_nt(source, flat), 32, 8)
            kept = jnp.where((lane & 7) < ncs[0, l], kept, 0.0).astype(BF)
            nr[j, :, 512 * l2 : 512 * l2 + 256] = kept[0:16]
            nr[j, :, 512 * l2 + 256 : 512 * l2 + 512] = kept[16:32]
        return 0

    lax.fori_loop(0, 8, near_pair, 0)

    for copy in p1_copies:
        copy.wait_recv()
    for copy in idx_copies:
        copy.wait_recv()
    to_smem = pltpu.make_async_copy(idxv, idxs, load_sem.at[13])
    to_smem.start()
    for j in range(4):
        place = place_matrix(j)
        for zl in range(2):
            m = 4 * zl + j
            wide = dot_nn(p1[m].reshape(128, 128), place).astype(BF)
            for quad in range(8):
                for a in range(4):
                    r2[32 * m + 4 * quad + a] = wide[
                        16 * quad : 16 * quad + 16, 128 * a : 128 * a + 128
                    ]
    to_smem.wait()
    p2_copies = []
    for o in list(range(1, 16)) + [0]:
        slot = ((4 - (o >> 2)) % 4) * 4 + (4 - (o & 3)) % 4
        for zl in range(2):
            first = zhi * 32 + zl * 16 + yhi * 4
            tile = r2[32 * (4 * zl) + idxs[slot, 0, first]]
            for j in range(1, 4):
                tile = tile + r2[32 * (4 * zl + j) + idxs[slot, 0, first + j]]
            if o == 0:
                fbuf[zhi, zl, yhi] = tile
            else:
                send[o, zl] = tile
        if o:
            p2_copies.append(
                remote(
                    send.at[o],
                    fbuf.at[zhi, :, yhi],
                    p2_ssem.at[o],
                    p2_rsem.at[o],
                    far_peer(o),
                )
            )

    lax.fori_loop(8, 16, near_pair, 0)
    row, col = iotas((1024, 128))
    group = row >> 8
    fold_near = ones_where(col == (group >> 1) * 64 + ((row & 255) >> 3) * 2 + (group & 1))
    nf[...] = dot_nn(nr[...].reshape(256, 1024), fold_near)

    for copy in pw_copies:
        copy.wait_recv()
    wide = dot_nn(pw[...].reshape(256, 128), spread).astype(BF)
    for device in range(16):
        for c in range(4):
            tp[4 * device + c] = wide[16 * device : 16 * device + 16, 128 * c : 128 * c + 128]
    for copy in cb_copies:
        copy.wait_recv()
    loads["coarse_far"].wait()
    loads["coarse_count"].wait()
    total = jnp.zeros((16, 128), F32)
    sub, _ = iotas((8, 1024))
    row, col = iotas((256, 128))
    for cp in range(2):
        counts = jnp.where(sub < 4, ccs[0, 2 * cp], ccs[0, 2 * cp + 1])
        product = jnp.zeros((128, 256), F32)
        for gp in range(2):
            halves = []
            for g in (2 * gp, 2 * gp + 1):
                rows = jnp.concatenate(
                    [cb[g, 2 * cp].astype(F32), cb[g, 2 * cp + 1].astype(F32)], axis=0
                )
                rows = jnp.where((sub & 3) + 4 * g < counts, rows, 0.0)
                halves.append(expand(lane_tiles(rows)))
            weights = jnp.concatenate(halves, axis=1)
            source = jnp.concatenate(
                [
                    jnp.concatenate(
                        [
                            tp[cfs[2 * cp + (k >> 2), 4 * g + (k & 3)] & 63]
                            for g in (2 * gp, 2 * gp + 1)
                        ],
                        axis=1,
                    )
                    for k in range(8)
                ],
                axis=0,
            )
            product += dot_nt(source, weights)
        kept = diagonal(product, 16, 8).astype(BF)
        target = (2 * cp + ((row & 7) >> 2)) * 32 + (row >> 3)
        total += dot_nn(kept, ones_where(col == target))
    field = total.astype(BF)

    row, col = iotas((128, 256))
    flat = jnp.concatenate(lane_tiles(trn[...]), axis=0)
    spreads = []
    for r4 in range(4):
        hit = ((row >> 5) == ((col & 31) >> 3)) & (((row & 31) >> 2) == (col >> 5))
        spreads.append(dot_nn(field, ones_where(hit & ((row & 3) == r4))).astype(BF))
    _, lane = iotas((16, 256))
    _, col = iotas((16, 128))
    for part in range(4):
        pieces = []
        for l in range(8 * part, 8 * part + 8):
            mask = ones_where((lane & 31) == l)
            pieces += [spreads[r4] * mask for r4 in range(4)]
        product = dot_nn(jnp.concatenate(pieces, axis=0), flat)
        for i in range(8):
            kept = product[64 * i : 64 * i + 16]
            for r4 in range(1, 4):
                at = 64 * i + 16 * r4
                kept = jnp.where((col >> 5) == r4, product[at : at + 16], kept)
            dr[8 * part + i] = kept.astype(BF)

    loads["far_slots"].wait()
    for copy in p2_copies:
        copy.wait_recv()
    wide = dot_nn(fbuf[...].reshape(512, 128), spread).astype(BF)
    for quad in range(32):
        for a in range(4):
            tt[4 * quad + a] = wide[16 * quad : 16 * quad + 16, 128 * a : 128 * a + 128]

    def far_part(step, _):
        for i in range(4):
            l = 4 * step + i
            source = jnp.concatenate(
                [
                    jnp.concatenate([tt[fss[k, l]], tt[fss[k + 8, l]]], axis=1)
                    for k in range(8)
                ],
                axis=0,
            )
            fr[l] = diagonal(dot_nt(source, bx[l]), 16, 8).astype(BF)
        return 0

    lax.fori_loop(0, 8, far_part, 0)

    row, col = iotas((256, 32))
    local = dot_nn(fr[...].reshape(512, 256), ones_where(col == (row >> 3)))
    row, col = iotas((128, 32))
    local += dot_nn(dr[...].reshape(512, 128), ones_where(col == (row & 31)))
    local = local.astype(BF)
    _, col = iotas((16, 128))
    for j in range(16):
        both = dot_nn(local[32 * j : 32 * j + 32], bas[:, 128 * j : 128 * j + 128])
        field = jnp.where(col < 64, both[0:16], both[16:32])
        out_ref[:, 128 * j : 128 * j + 128] = (field + nf[16 * j : 16 * j + 16]).astype(BF)

    for copy in sends:
        copy.wait_send()


def per_device(
    points_in,
    leaf_basis,
    transfer,
    far_blocks,
    near_blocks,
    near_leaf,
    near_count,
    far_slots,
    far_count,
    recv_rows,
    coarse_blocks,
    coarse_far,
    coarse_count,
):
    vmem = pltpu.VMEM
    smem = pltpu.SMEM
    dma = pltpu.SemaphoreType.DMA
    anywhere = pl.BlockSpec(memory_space=pltpu.HBM)
    return pl.pallas_call(
        kernel,
        out_shape=jax.ShapeDtypeStruct((16, 2048), BF),
        in_specs=[anywhere] * 13,
        out_specs=pl.BlockSpec(memory_space=pltpu.VMEM),
        scratch_shapes=[
            vmem((16, 2048), BF),
            vmem((32, 2048), BF),
            vmem((32, 1024), BF),
            vmem((32, 16, 1024), BF),
            vmem((32, 8, 4096), BF),
            vmem((4, 4, 4, 1024), BF),
            vmem((2, 16, 256), BF),
            vmem((8, 8, 16, 128), BF),
            vmem((32, 16, 128), BF),
            vmem((16, 16, 128), BF),
            vmem((64, 16, 128), BF),
            vmem((256, 16, 128), BF),
            vmem((16, 2, 16, 128), BF),
            vmem((4, 2, 4, 16, 128), BF),
            vmem((128, 16, 128), BF),
            vmem((32, 256, 256), BF),
            vmem((40, 32, 128), BF),
            vmem((16, 16, 1024), BF),
            vmem((256, 128), F32),
            vmem((32, 16, 256), BF),
            vmem((32, 16, 128), BF),
            vmem((16, 1, 128), jnp.int32),
            smem((16, 1, 128), jnp.int32),
            smem((8, 32), jnp.int32),
            smem((1, 32), jnp.int32),
            smem((16, 32), jnp.int32),
            smem((1, 32), jnp.int32),
            smem((4, 16), jnp.int32),
            smem((1, 4), jnp.int32),
            dma((14,)),
            dma((16,)),
            dma((16,)),
            dma((8,)),
            dma((8,)),
            dma((16,)),
            dma((16,)),
            dma((16,)),
            dma((16,)),
            dma((2,)),
            dma((2,)),
            dma((4,)),
            dma((4,)),
        ],
        compiler_params=pltpu.CompilerParams(
            collective_id=0, has_side_effects=True, vmem_limit_bytes=63 * 1024 * 1024
        ),
        cost_estimate=pl.CostEstimate(
            flops=60_000_000, bytes_accessed=3_600_000, transcendentals=0
        ),
    )(
        points_in,
        leaf_basis,
        transfer,
        far_blocks,
        near_blocks,
        near_leaf.T,
        near_count.reshape(1, 32),
        far_slots.T,
        far_count.reshape(1, 32),
        recv_rows.reshape(1, 128),
        coarse_blocks,
        coarse_far,
        coarse_count.reshape(1, 4),
    )


def solution(mesh):
    in_specs = (
        P("grp", "leaf"),
        P(None, "leaf"),
        P("leaf", None),
        P("leaf", None, None),
        P("leaf", None, None),
        P("leaf", None),
        P("leaf"),
        P("leaf", None),
        P("leaf"),
        P("leaf", None, None),
        P("leaf", "grp", None),
        P("leaf", None),
        P("leaf"),
    )
    out_specs = P("grp", "leaf")
    return jax.shard_map(
        per_device, mesh=mesh, in_specs=in_specs, out_specs=out_specs, check_vma=False
    )
```

time: 124 us -> 40.1 us (0.32)
  the two profiles are of different devices: /device:TPU:1 before, /device:TPU:6 now
where the time goes in v1:
time: 40.1 us; the launch traced here: 39.9 us
  Pallas kernels  38.4 us (96%)
  local copies, waits for them, and re-layouts  1.47 us (4%)
    pallas_call x1, Pallas kernels, per_device(): pl.pallas_call(kernel, out_shape=jax.ShapeDtypeStruct((16, 2048), BF), in...  38.4 us
    unnamed x1, local copies, waits for them, and re-layouts  1.47 us

profile of v1, /device:TPU:6, one launch (start us, length us, event | category | flops | bytes accessed | tf_op | source)
XLA Modules:
  0.0 39.9 jit_solution(8918427887237535984)
XLA Ops:
  0.0 38.4 %shard_map.127 = bf16[16,2048]{1,0:T(8,128)(2,1)} custom-call(bf16[16,2048]{1,0:T(8,128)(2,1)} %points_h.1, bf16[32,2048]{1,0:T(8,128)(2,1)} %basis_h.1, bf16[32,1024]{1,0:T(8,128)(2,1)} %transfer_h.1, bf16[32,16,1024]{2,1,0:T(8,128)(2,1)} %far_h.1, bf16[32,8,4096]{2,1,0:T(8,128)(2,1)} %near_h.1, s32[8,32]{1,0:T(8,128)} %bitcast.7, s32[1,32]{1,0:T(1,128)} %bitcast.8, ...), custom_call_target="tpu_custom_call" | custom-call | flops 60000000 | bytes 3600000 | tf_op jit(solution)/shard_map/pallas_call | solution.py:463
  38.5 1.5 %copy.15 = bf16[16,2048]{1,0:T(8,128)(2,1)} copy(bf16[16,2048]{1,0:T(8,128)(2,1)} %shard_map.127) | data formatting | bytes 131072

commit v2 on v1

--- a/solution.py
+++ b/solution.py
@@ -117,26 +117,36 @@
     me = lax.axis_index("leaf")
     grp = lax.axis_index("grp")
     core = lax.rem(me, 2)
-    ylo = lax.rem(lax.div(me, 2), 2)
-    yhi = lax.rem(lax.div(me, 4), 4)
-    zlo = lax.rem(lax.div(me, 16), 2)
-    zhi = lax.div(me, 32)
-    member = zlo * 4 + ylo * 2 + core
+    y = lax.rem(lax.div(me, 2), 8)
+    z = lax.div(me, 16)
     in_group = lax.rem(me, 16)
-
-    def cube_peer(o):
-        c = lax.rem(core + (o & 1), 2)
-        y = lax.rem(ylo + ((o >> 1) & 1), 2)
-        z = lax.rem(zlo + ((o >> 2) & 1), 2)
-        return (zhi * 32 + z * 16 + yhi * 4 + y * 2 + c, grp)
-
-    def far_peer(o):
-        z = lax.rem(zhi + (o >> 2), 4)
-        y = lax.rem(yhi + (o & 3), 4)
-        return (z * 32 + zlo * 16 + y * 4 + ylo * 2 + core, grp)
+    place = (1 - core) * z + core * y
+    line = (1 - core) * y + core * z
+    own_server = core * 8 + line
+    own_client = line * 2 + core
+
+    def line_peer(o):
+        turned = lax.rem(place + o, 8)
+        return ((1 - core) * (turned * 16 + y * 2) + core * (z * 16 + turned * 2 + 1), grp)
+
+    def server(m):
+        kind, at = lax.div(m, 8), lax.rem(m, 8)
+        return ((1 - kind) * (z * 16 + at * 2) + kind * (at * 16 + y * 2 + 1), grp)
+
+    def client_slot(m):
+        kind = lax.div(m, 8)
+        return ((1 - kind) * y + kind * z) * 2 + core
+
+    def client(slot):
+        at, c = lax.div(slot, 2), lax.rem(slot, 2)
+        return ((1 - core) * (z * 16 + at * 2) + core * (at * 16 + y * 2) + c, grp)
 
     def group_peer(o):
-        return (lax.div(me, 16) * 16 + lax.rem(in_group + o, 16), grp)
+        return (z * 16 + lax.rem(in_group + o, 16), grp)
+
+    def column_peer(o):
+        turned = lax.rem(z + (o >> 1), 8)
+        return (turned * 16 + y * 2 + lax.rem(core + (o & 1), 2), grp)
 
     up = (lax.rem(me + 1, 128), grp)
     down = (lax.rem(me + 127, 128), grp)
@@ -153,13 +163,12 @@
     load("points", points_h, pts, 0)
     load("basis", basis_h, bas, 1)
     load("transfer", transfer_h, trn, 2)
-    load("recv", recv_h, idxv.at[0], 3)
+    load("recv", recv_h, idxv.at[own_client], 3)
     load("coarse", coarse_h, cb.at[grp], 4)
 
     barrier = pltpu.get_barrier_semaphore()
-    peers = [cube_peer(o) for o in range(1, 8)]
-    peers += [far_peer(o) for o in range(1, 16)]
-    peers += [group_peer(o) for o in range(1, 16)]
+    peers = [group_peer(o) for o in range(1, 16)]
+    peers += [column_peer(o) for o in range(2, 16)]
     peers += [up, down]
     peers += [grp_peer(o) for o in range(1, 4)]
     for peer in peers:
@@ -182,10 +191,61 @@
         lanes = slice(256 * quad, 256 * quad + 256)
         v = bas[:, lanes]
         vv = jnp.concatenate([v * mask for mask in quad_masks], axis=0)
-        p1[member, quad] = dot_nt(pts[:, lanes], vv).astype(BF)
+        p1[place, quad] = dot_nt(pts[:, lanes], vv).astype(BF)
+
+    loads["recv"].wait()
+    loads["coarse"].wait()
+    pl.semaphore_wait(barrier, len(peers))
+
+    sends = []
+
+    def remote(src, dst, ssem, rsem, peer):
+        copy = pltpu.make_async_remote_copy(
+            src_ref=src,
+            dst_ref=dst,
+            send_sem=ssem,
+            recv_sem=rsem,
+            device_id=peer,
+            device_id_type=MESH,
+        )
+        copy.start()
+        sends.append(copy)
+        return copy
+
+    p1_copies = [
+        remote(
+            p1.at[place],
+            p1.at[place],
+            p1_ssem.at[o],
+            p1_rsem.at[o],
+            line_peer(o),
+        )
+        for o in range(1, 8)
+    ]
+    idx_copies = []
+    for o in range(1, 16):
+        m = lax.rem(own_server + o, 16)
+        slot = client_slot(m)
+        idx_copies.append(
+            remote(
+                idxv.at[own_client],
+                idxv.at[slot],
+                idx_ssem.at[o],
+                idx_rsem.at[slot],
+                server(m),
+            )
+        )
+    halo_copies = [
+        remote(pts.at[:, pl.ds(1792, 256)], halo.at[0], halo_ssem.at[0], halo_rsem.at[0], up),
+        remote(pts.at[:, pl.ds(0, 256)], halo.at[1], halo_ssem.at[1], halo_rsem.at[1], down),
+    ]
+    cb_copies = [
+        remote(cb.at[grp], cb.at[grp], cb_ssem.at[o], cb_rsem.at[o], grp_peer(o))
+        for o in range(1, 4)
+    ]
 
     spread = spread_matrix()
-    wide = dot_nn(p1[member].reshape(128, 128), spread).astype(BF)
+    wide = dot_nn(p1[place].reshape(128, 128), spread).astype(BF)
     for quad in range(8):
         for a in range(4):
             rown[4 * quad + a] = wide[16 * quad : 16 * quad + 16, 128 * a : 128 * a + 128]
@@ -199,44 +259,9 @@
         total += dot_nn(kept, ones_where(col == c * 32 + (row >> 3)))
     pw[in_group] = total.astype(BF)
 
-    loads["recv"].wait()
-    loads["coarse"].wait()
-    pl.semaphore_wait(barrier, len(peers))
-
-    sends = []
-
-    def remote(src, dst, ssem, rsem, peer):
-        copy = pltpu.make_async_remote_copy(
-            src_ref=src,
-            dst_ref=dst,
-            send_sem=ssem,
-            recv_sem=rsem,
-            device_id=peer,
-            device_id_type=MESH,
-        )
-        copy.start()
-        sends.append(copy)
-        return copy
-
-    p1_copies = [
-        remote(p1.at[member], p1.at[member], p1_ssem.at[o], p1_rsem.at[o], cube_peer(o))
-        for o in range(1, 8)
-    ]
-    idx_copies = [
-        remote(idxv.at[0], idxv.at[o], idx_ssem.at[o], idx_rsem.at[o], far_peer(o))
-        for o in range(1, 16)
-    ]
-    halo_copies = [
-        remote(pts.at[:, pl.ds(1792, 256)], halo.at[0], halo_ssem.at[0], halo_rsem.at[0], up),
-        remote(pts.at[:, pl.ds(0, 256)], halo.at[1], halo_ssem.at[1], halo_rsem.at[1], down),
-    ]
     pw_copies = [
         remote(pw.at[in_group], pw.at[in_group], pw_ssem.at[o], pw_rsem.at[o], group_peer(o))
         for o in range(1, 16)
-    ]
-    cb_copies = [
-        remote(cb.at[grp], cb.at[grp], cb_ssem.at[o], cb_rsem.at[o], grp_peer(o))
-        for o in range(1, 4)
     ]
 
     loads["far"].wait()
@@ -285,50 +310,55 @@
                 [tn[jnp.clip(nls[k, l] - me * 32 + 4, 0, 39)] for k in range(8)], axis=0
             )
             kept = diagonal(dot_nt(source, flat), 32, 8)
-            kept = jnp.where((lane & 7) < ncs[0, l], kept, 0.0).astype(BF)
-            nr[j, :, 512 * l2 : 512 * l2 + 256] = kept[0:16]
-            nr[j, :, 512 * l2 + 256 : 512 * l2 + 512] = kept[16:32]
+            kept = jnp.where((lane & 7) < ncs[0, l], kept, 0.0)
+            high = kept.astype(BF)
+            for part, value in enumerate([high, (kept - high.astype(F32)).astype(BF)]):
+                nr[part, j, :, 512 * l2 : 512 * l2 + 256] = value[0:16]
+                nr[part, j, :, 512 * l2 + 256 : 512 * l2 + 512] = value[16:32]
         return 0
 
     lax.fori_loop(0, 8, near_pair, 0)
 
     for copy in p1_copies:
         copy.wait_recv()
-    for copy in idx_copies:
-        copy.wait_recv()
+    for o in range(1, 16):
+        slot = lax.rem(own_client + o, 16)
+        pltpu.make_async_copy(idxv.at[slot], idxv.at[slot], idx_rsem.at[slot]).wait()
     to_smem = pltpu.make_async_copy(idxv, idxs, load_sem.at[13])
     to_smem.start()
     for j in range(4):
-        place = place_matrix(j)
-        for zl in range(2):
-            m = 4 * zl + j
-            wide = dot_nn(p1[m].reshape(128, 128), place).astype(BF)
+        place_j = place_matrix(j)
+        for g in range(2):
+            m = 4 * g + j
+            wide = dot_nn(p1[m].reshape(128, 128), place_j).astype(BF)
             for quad in range(8):
                 for a in range(4):
                     r2[32 * m + 4 * quad + a] = wide[
                         16 * quad : 16 * quad + 16, 128 * a : 128 * a + 128
                     ]
     to_smem.wait()
+    first = (1 - core) * (y * 2) + core * (z * 16 + 1)
+    stride = (1 - core) * 16 + core * 2
     p2_copies = []
     for o in list(range(1, 16)) + [0]:
-        slot = ((4 - (o >> 2)) % 4) * 4 + (4 - (o & 3)) % 4
-        for zl in range(2):
-            first = zhi * 32 + zl * 16 + yhi * 4
-            tile = r2[32 * (4 * zl) + idxs[slot, 0, first]]
+        slot = lax.rem(own_client + o, 16)
+        for g in range(2):
+            tile = r2[32 * (4 * g) + idxs[slot, 0, first + 4 * g * stride]]
             for j in range(1, 4):
-                tile = tile + r2[32 * (4 * zl + j) + idxs[slot, 0, first + j]]
+                m = 4 * g + j
+                tile = tile + r2[32 * m + idxs[slot, 0, first + m * stride]]
             if o == 0:
-                fbuf[zhi, zl, yhi] = tile
+                fbuf[own_server, g] = tile
             else:
-                send[o, zl] = tile
+                send[o, g] = tile
         if o:
             p2_copies.append(
                 remote(
                     send.at[o],
-                    fbuf.at[zhi, :, yhi],
+                    fbuf.at[own_server],
                     p2_ssem.at[o],
-                    p2_rsem.at[o],
-                    far_peer(o),
+                    p2_rsem.at[own_server],
+                    client(slot),
                 )
             )
 
@@ -336,7 +366,8 @@
     row, col = iotas((1024, 128))
     group = row >> 8
     fold_near = ones_where(col == (group >> 1) * 64 + ((row & 255) >> 3) * 2 + (group & 1))
-    nf[...] = dot_nn(nr[...].reshape(256, 1024), fold_near)
+    nf[...] = dot_nn(nr[0].reshape(256, 1024), fold_near)
+    nf[...] += dot_nn(nr[1].reshape(256, 1024), fold_near)
 
     for copy in pw_copies:
         copy.wait_recv()
@@ -404,12 +435,17 @@
             dr[8 * part + i] = kept.astype(BF)
 
     loads["far_slots"].wait()
-    for copy in p2_copies:
-        copy.wait_recv()
+    for o in range(1, 16):
+        m = lax.rem(own_server + o, 16)
+        pltpu.make_async_copy(fbuf.at[m], fbuf.at[m], p2_rsem.at[m]).wait()
     wide = dot_nn(fbuf[...].reshape(512, 128), spread).astype(BF)
-    for quad in range(32):
-        for a in range(4):
-            tt[4 * quad + a] = wide[16 * quad : 16 * quad + 16, 128 * a : 128 * a + 128]
+    for m in range(16):
+        for i in range(8):
+            kind, at = divmod(m, 8)
+            f = at * 16 + i * 2 + 1 if kind else i * 16 + at * 2
+            row = 32 * m + 16 * (i // 4)
+            lane = 128 * (i % 4)
+            tt[f] = wide[row : row + 16, lane : lane + 128]
 
     def far_part(step, _):
         for i in range(4):
@@ -479,11 +515,11 @@
             vmem((64, 16, 128), BF),
             vmem((256, 16, 128), BF),
             vmem((16, 2, 16, 128), BF),
-            vmem((4, 2, 4, 16, 128), BF),
+            vmem((16, 2, 16, 128), BF),
             vmem((128, 16, 128), BF),
             vmem((32, 256, 256), BF),
             vmem((40, 32, 128), BF),
-            vmem((16, 16, 1024), BF),
+            vmem((2, 16, 16, 1024), BF),
             vmem((256, 128), F32),
             vmem((32, 16, 256), BF),
             vmem((32, 16, 128), BF),

time: 40.1 us -> 34.4 us (0.86)
  the two profiles are of different devices: /device:TPU:6 before, /device:TPU:1 now
where the time goes in v2:
time: 34.4 us; the launch traced here: 34.3 us
  Pallas kernels  32.8 us (95%)
  local copies, waits for them, and re-layouts  1.47 us (4%)
    pallas_call x1, Pallas kernels, per_device(): pl.pallas_call(kernel, out_shape=jax.ShapeDtypeStruct((16, 2048), BF), in...  32.8 us
    unnamed x1, local copies, waits for them, and re-layouts  1.47 us

profile of v2, /device:TPU:1, one launch (start us, length us, event | category | flops | bytes accessed | tf_op | source)
XLA Modules:
  0.0 34.3 jit_solution(6846235858907764372)
XLA Ops:
  0.0 32.8 %shard_map.127 = bf16[16,2048]{1,0:T(8,128)(2,1)} custom-call(bf16[16,2048]{1,0:T(8,128)(2,1)} %points_h.1, bf16[32,2048]{1,0:T(8,128)(2,1)} %basis_h.1, bf16[32,1024]{1,0:T(8,128)(2,1)} %transfer_h.1, bf16[32,16,1024]{2,1,0:T(8,128)(2,1)} %far_h.1, bf16[32,8,4096]{2,1,0:T(8,128)(2,1)} %near_h.1, s32[8,32]{1,0:T(8,128)} %bitcast.7, s32[1,32]{1,0:T(1,128)} %bitcast.8, ...), custom_call_target="tpu_custom_call" | custom-call | flops 60000000 | bytes 3600000 | tf_op jit(solution)/shard_map/pallas_call | solution.py:499
  32.8 1.5 %copy.15 = bf16[16,2048]{1,0:T(8,128)(2,1)} copy(bf16[16,2048]{1,0:T(8,128)(2,1)} %shard_map.127) | data formatting | bytes 131072

commit v3 on v2

--- a/solution.py
+++ b/solution.py
@@ -86,12 +86,14 @@
     send,
     fbuf,
     tt,
-    bx,
+    wf,
+    vf,
+    bs,
     tn,
     nr,
     nf,
-    fr,
     dr,
+    dn,
     idxv,
     idxs,
     nls,
@@ -180,8 +182,8 @@
     load("far_count", far_count_h, fcs, 8)
     load("coarse_far", coarse_far_h, cfs, 9)
     load("coarse_count", coarse_count_h, ccs, 10)
+    load("far", far_h, farv, 12)
     load("near", near_h, nearv, 11)
-    load("far", far_h, farv, 12)
 
     loads["points"].wait()
     loads["basis"].wait()
@@ -191,10 +193,43 @@
         lanes = slice(256 * quad, 256 * quad + 256)
         v = bas[:, lanes]
         vv = jnp.concatenate([v * mask for mask in quad_masks], axis=0)
-        p1[place, quad] = dot_nt(pts[:, lanes], vv).astype(BF)
+        p1[0, quad] = dot_nt(pts[:, lanes], vv).astype(BF)
 
     loads["recv"].wait()
     loads["coarse"].wait()
+    def prepare(quad, _):
+        sub, _ = iotas((16, 1024))
+        for l4 in range(4):
+            l = 4 * quad + l4
+            blocks = jnp.where(sub < fcs[0, l], farv[l].astype(F32), 0.0)
+            for t, tile in enumerate(lane_tiles(blocks)):
+                bs[pl.ds((8 * l4 + t) * 16, 16), :] = tile
+        _, col = iotas((32, 128))
+        masks = [jnp.where((col >> 5) == r4, 1.0, 0.0) for r4 in range(4)]
+        row, col = iotas((32, 128))
+        gather = ones_where((col & 31) == row)
+        for k in range(16):
+            tile = bs[pl.ds(k, 32, stride=16), :]
+            rows = jnp.concatenate([tile * mask for mask in masks], axis=0).astype(BF)
+            wf[quad, 32 * k : 32 * k + 32, :] = dot_nt(gather, rows).astype(BF)
+        return 0
+
+    def prepare_all():
+        loads["far"].wait()
+        loads["far_count"].wait()
+        lax.fori_loop(0, 8, prepare, 0)
+        row, col = iotas((128, 32))
+        permute = ones_where(col == 4 * (row & 7) + (row >> 5))
+        row, col = iotas((128, 256))
+        block = ((row >> 3) & 3) == (col >> 6)
+        for quad in range(8):
+            rows = dot_nn(permute, bas[:, 256 * quad : 256 * quad + 256])
+            vf[quad] = jnp.where(block, rows, 0.0).astype(BF)
+
+    @pl.when(z < 4)
+    def _():
+        prepare_all()
+
     pl.semaphore_wait(barrier, len(peers))
 
     sends = []
@@ -212,16 +247,16 @@
         sends.append(copy)
         return copy
 
-    p1_copies = [
-        remote(
-            p1.at[place],
-            p1.at[place],
+    p1_copies = {
+        8 - o: remote(
+            p1.at[0],
+            p1.at[8 - o],
             p1_ssem.at[o],
-            p1_rsem.at[o],
+            p1_rsem.at[8 - o],
             line_peer(o),
         )
-        for o in range(1, 8)
-    ]
+        for o in (4, 3, 5, 2, 6, 1, 7)
+    }
     idx_copies = []
     for o in range(1, 16):
         m = lax.rem(own_server + o, 16)
@@ -245,7 +280,7 @@
     ]
 
     spread = spread_matrix()
-    wide = dot_nn(p1[place].reshape(128, 128), spread).astype(BF)
+    wide = dot_nn(p1[0].reshape(128, 128), spread).astype(BF)
     for quad in range(8):
         for a in range(4):
             rown[4 * quad + a] = wide[16 * quad : 16 * quad + 16, 128 * a : 128 * a + 128]
@@ -264,20 +299,9 @@
         for o in range(1, 16)
     ]
 
-    loads["far"].wait()
-    loads["far_count"].wait()
-
-    def prepare(l, _):
-        count = fcs[0, l]
-        sub, _ = iotas((8, 128))
-        low = jnp.where(sub < count, 1.0, 0.0)
-        high = jnp.where(sub + 8 < count, 1.0, 0.0)
-        blocks = farv[l].astype(F32)
-        bx[l, :, 0:128] = expand([tile * low for tile in lane_tiles(blocks[0:8])])
-        bx[l, :, 128:256] = expand([tile * high for tile in lane_tiles(blocks[8:16])])
-        return 0
-
-    lax.fori_loop(0, 32, prepare, 0)
+    @pl.when(z >= 4)
+    def _():
+        prepare_all()
 
     _, col = iotas((16, 128))
     left = jnp.where(col < 64, 1.0, 0.0)
@@ -319,34 +343,33 @@
 
     lax.fori_loop(0, 8, near_pair, 0)
 
-    for copy in p1_copies:
-        copy.wait_recv()
     for o in range(1, 16):
         slot = lax.rem(own_client + o, 16)
         pltpu.make_async_copy(idxv.at[slot], idxv.at[slot], idx_rsem.at[slot]).wait()
     to_smem = pltpu.make_async_copy(idxv, idxs, load_sem.at[13])
     to_smem.start()
-    for j in range(4):
-        place_j = place_matrix(j)
-        for g in range(2):
-            m = 4 * g + j
-            wide = dot_nn(p1[m].reshape(128, 128), place_j).astype(BF)
-            for quad in range(8):
-                for a in range(4):
-                    r2[32 * m + 4 * quad + a] = wide[
-                        16 * quad : 16 * quad + 16, 128 * a : 128 * a + 128
-                    ]
+    for i in (0, 1, 2, 3, 7, 5, 4, 6):
+        if i:
+            p1_copies[i].wait_recv()
+        wide = dot_nn(p1[i].reshape(128, 128), place_matrix(i % 4)).astype(BF)
+        for quad in range(8):
+            for a in range(4):
+                r2[32 * i + 4 * quad + a] = wide[
+                    16 * quad : 16 * quad + 16, 128 * a : 128 * a + 128
+                ]
     to_smem.wait()
-    first = (1 - core) * (y * 2) + core * (z * 16 + 1)
-    stride = (1 - core) * 16 + core * 2
+    owners = []
+    for i in range(8):
+        turned = lax.rem(place + i, 8)
+        owners.append((1 - core) * (turned * 16 + y * 2) + core * (z * 16 + turned * 2 + 1))
     p2_copies = []
-    for o in list(range(1, 16)) + [0]:
+    for o in (8, 9, 7, 10, 6, 11, 5, 12, 4, 13, 3, 14, 2, 15, 1, 0):
         slot = lax.rem(own_client + o, 16)
         for g in range(2):
-            tile = r2[32 * (4 * g) + idxs[slot, 0, first + 4 * g * stride]]
+            tile = r2[32 * (4 * g) + idxs[slot, 0, owners[4 * g]]]
             for j in range(1, 4):
                 m = 4 * g + j
-                tile = tile + r2[32 * m + idxs[slot, 0, first + m * stride]]
+                tile = tile + r2[32 * m + idxs[slot, 0, owners[m]]]
             if o == 0:
                 fbuf[own_server, g] = tile
             else:
@@ -432,46 +455,46 @@
             for r4 in range(1, 4):
                 at = 64 * i + 16 * r4
                 kept = jnp.where((col >> 5) == r4, product[at : at + 16], kept)
-            dr[8 * part + i] = kept.astype(BF)
+            l = 8 * part + i
+            dr[l // 4, :, 128 * (l % 4) : 128 * (l % 4) + 128] = kept.astype(BF)
+    row, col = iotas((512, 128))
+    hit = ((row >> 7) == ((col >> 3) & 3)) & ((row & 31) == 4 * (col & 7) + (col >> 5))
+    dn[...] = dot_nn(dr[...].reshape(128, 512), ones_where(hit))
 
     loads["far_slots"].wait()
-    for o in range(1, 16):
+    for o in range(16):
         m = lax.rem(own_server + o, 16)
-        pltpu.make_async_copy(fbuf.at[m], fbuf.at[m], p2_rsem.at[m]).wait()
-    wide = dot_nn(fbuf[...].reshape(512, 128), spread).astype(BF)
-    for m in range(16):
+        if o:
+            pltpu.make_async_copy(fbuf.at[m], fbuf.at[m], p2_rsem.at[m]).wait()
+        kind, at = lax.div(m, 8), lax.rem(m, 8)
+        wide = dot_nn(fbuf[m].reshape(32, 128), spread).astype(BF)
         for i in range(8):
-            kind, at = divmod(m, 8)
-            f = at * 16 + i * 2 + 1 if kind else i * 16 + at * 2
-            row = 32 * m + 16 * (i // 4)
-            lane = 128 * (i % 4)
+            row_owner = lax.rem(z + i, 8) * 16 + at * 2
+            column_owner = at * 16 + lax.rem(y + i, 8) * 2 + 1
+            f = (1 - kind) * row_owner + kind * column_owner
+            row, lane = 16 * (i // 4), 128 * (i % 4)
             tt[f] = wide[row : row + 16, lane : lane + 128]
-
-    def far_part(step, _):
-        for i in range(4):
-            l = 4 * step + i
-            source = jnp.concatenate(
-                [
-                    jnp.concatenate([tt[fss[k, l]], tt[fss[k + 8, l]]], axis=1)
-                    for k in range(8)
-                ],
-                axis=0,
-            )
-            fr[l] = diagonal(dot_nt(source, bx[l]), 16, 8).astype(BF)
-        return 0
-
-    lax.fori_loop(0, 8, far_part, 0)
-
-    row, col = iotas((256, 32))
-    local = dot_nn(fr[...].reshape(512, 256), ones_where(col == (row >> 3)))
-    row, col = iotas((128, 32))
-    local += dot_nn(dr[...].reshape(512, 128), ones_where(col == (row & 31)))
-    local = local.astype(BF)
     _, col = iotas((16, 128))
-    for j in range(16):
-        both = dot_nn(local[32 * j : 32 * j + 32], bas[:, 128 * j : 128 * j + 128])
-        field = jnp.where(col < 64, both[0:16], both[16:32])
-        out_ref[:, 128 * j : 128 * j + 128] = (field + nf[16 * j : 16 * j + 16]).astype(BF)
+    parts = [ones_where((col >> 5) == j) for j in range(4)]
+    for quad in range(8):
+        rows = []
+        for l in range(4 * quad, 4 * quad + 4):
+            tiles = []
+            for k in range(0, 16, 4):
+                tile = tt[fss[k, l]] * parts[0]
+                for j in range(1, 4):
+                    tile = tile + tt[fss[k + j, l]] * parts[j]
+                tiles.append(tile)
+            rows.append(jnp.concatenate(tiles, axis=1))
+        product = dot_nn(jnp.concatenate(rows, axis=0), wf[quad])
+        local = product[0:16]
+        for l4 in range(1, 4):
+            local = jnp.where(((col >> 3) & 3) == l4, product[16 * l4 : 16 * l4 + 16], local)
+        local = (local + dn[16 * quad : 16 * quad + 16]).astype(BF)
+        near = jnp.concatenate(
+            [nf[32 * quad : 32 * quad + 16], nf[32 * quad + 16 : 32 * quad + 32]], axis=1
+        )
+        out_ref[:, 256 * quad : 256 * quad + 256] = (dot_nn(local, vf[quad]) + near).astype(BF)
 
     for copy in sends:
         copy.wait_send()
@@ -517,12 +540,14 @@
             vmem((16, 2, 16, 128), BF),
             vmem((16, 2, 16, 128), BF),
             vmem((128, 16, 128), BF),
-            vmem((32, 256, 256), BF),
+            vmem((8, 512, 128), BF),
+            vmem((8, 128, 256), BF),
+            vmem((512, 128), F32),
             vmem((40, 32, 128), BF),
             vmem((2, 16, 16, 1024), BF),
             vmem((256, 128), F32),
-            vmem((32, 16, 256), BF),
-            vmem((32, 16, 128), BF),
+            vmem((8, 16, 512), BF),
+            vmem((128, 128), F32),
             vmem((16, 1, 128), jnp.int32),
             smem((16, 1, 128), jnp.int32),
             smem((8, 32), jnp.int32),

time: 34.4 us -> 35.3 us (1.026)
  the two profiles are of different devices: /device:TPU:1 before, /device:TPU:4 now
where the time goes in v3:
time: 35.3 us; the launch traced here: 35.2 us
  Pallas kernels  33.7 us (95%)
  local copies, waits for them, and re-layouts  1.47 us (4%)
    pallas_call x1, Pallas kernels, per_device(): pl.pallas_call(kernel, out_shape=jax.ShapeDtypeStruct((16, 2048), BF), in...  33.7 us
    unnamed x1, local copies, waits for them, and re-layouts  1.47 us

profile of v3, /device:TPU:4, one launch (start us, length us, event | category | flops | bytes accessed | tf_op | source)
XLA Modules:
  0.0 35.2 jit_solution(12371744584922608122)
XLA Ops:
  0.0 33.7 %shard_map.127 = bf16[16,2048]{1,0:T(8,128)(2,1)} custom-call(bf16[16,2048]{1,0:T(8,128)(2,1)} %points_h.1, bf16[32,2048]{1,0:T(8,128)(2,1)} %basis_h.1, bf16[32,1024]{1,0:T(8,128)(2,1)} %transfer_h.1, bf16[32,16,1024]{2,1,0:T(8,128)(2,1)} %far_h.1, bf16[32,8,4096]{2,1,0:T(8,128)(2,1)} %near_h.1, s32[8,32]{1,0:T(8,128)} %bitcast.7, s32[1,32]{1,0:T(1,128)} %bitcast.8, ...), custom_call_target="tpu_custom_call" | custom-call | flops 60000000 | bytes 3600000 | tf_op jit(solution)/shard_map/pallas_call | solution.py:522
  33.7 1.5 %copy.15 = bf16[16,2048]{1,0:T(8,128)(2,1)} copy(bf16[16,2048]{1,0:T(8,128)(2,1)} %shard_map.127) | data formatting | bytes 131072

commit v4 on v3

--- a/solution.py
+++ b/solution.py
@@ -226,9 +226,45 @@
             rows = dot_nn(permute, bas[:, 256 * quad : 256 * quad + 256])
             vf[quad] = jnp.where(block, rows, 0.0).astype(BF)
 
+    _, col = iotas((16, 128))
+    left = jnp.where(col < 64, 1.0, 0.0)
+    right = 1.0 - left
+
+    def near_table(m, tile):
+        value = tile.astype(F32)
+        turned = pltpu.roll(value, 64, 1)
+        tn[m] = jnp.concatenate([value * left, turned * right], axis=0).astype(BF)
+        tn[m + 1] = jnp.concatenate([turned * left, value * right], axis=0).astype(BF)
+
+    def near_pair(j, _):
+        _, lane = iotas((32, 256))
+        for l2 in range(2):
+            l = 2 * j + l2
+            blocks = nearv[l].astype(F32)
+            flat = jnp.concatenate(lane_tiles(blocks), axis=0).astype(BF)
+            source = jnp.concatenate(
+                [tn[jnp.clip(nls[k, l] - me * 32 + 4, 0, 39)] for k in range(8)], axis=0
+            )
+            kept = diagonal(dot_nt(source, flat), 32, 8)
+            kept = jnp.where((lane & 7) < ncs[0, l], kept, 0.0)
+            high = kept.astype(BF)
+            for part, value in enumerate([high, (kept - high.astype(F32)).astype(BF)]):
+                nr[part, j, :, 512 * l2 : 512 * l2 + 256] = value[0:16]
+                nr[part, j, :, 512 * l2 + 256 : 512 * l2 + 512] = value[16:32]
+        return 0
+
+    def inner_work():
+        prepare_all()
+        for j in range(16):
+            near_table(4 + 2 * j, pts[:, 128 * j : 128 * j + 128])
+        loads["near"].wait()
+        loads["near_leaf"].wait()
+        loads["near_count"].wait()
+        lax.fori_loop(2, 14, near_pair, 0)
+
     @pl.when(z < 4)
     def _():
-        prepare_all()
+        inner_work()
 
     pl.semaphore_wait(barrier, len(peers))
 
@@ -299,64 +335,22 @@
         for o in range(1, 16)
     ]
 
-    @pl.when(z >= 4)
-    def _():
-        prepare_all()
-
-    _, col = iotas((16, 128))
-    left = jnp.where(col < 64, 1.0, 0.0)
-    right = 1.0 - left
-
-    def near_table(m, tile):
-        value = tile.astype(F32)
-        turned = pltpu.roll(value, 64, 1)
-        tn[m] = jnp.concatenate([value * left, turned * right], axis=0).astype(BF)
-        tn[m + 1] = jnp.concatenate([turned * left, value * right], axis=0).astype(BF)
-
-    for j in range(16):
-        near_table(4 + 2 * j, pts[:, 128 * j : 128 * j + 128])
-    for copy in halo_copies:
-        copy.wait_recv()
-    for j in range(2):
-        near_table(2 * j, halo[0, :, 128 * j : 128 * j + 128])
-        near_table(36 + 2 * j, halo[1, :, 128 * j : 128 * j + 128])
-    loads["near"].wait()
-    loads["near_leaf"].wait()
-    loads["near_count"].wait()
-
-    def near_pair(j, _):
-        _, lane = iotas((32, 256))
-        for l2 in range(2):
-            l = 2 * j + l2
-            blocks = nearv[l].astype(F32)
-            flat = jnp.concatenate(lane_tiles(blocks), axis=0).astype(BF)
-            source = jnp.concatenate(
-                [tn[jnp.clip(nls[k, l] - me * 32 + 4, 0, 39)] for k in range(8)], axis=0
-            )
-            kept = diagonal(dot_nt(source, flat), 32, 8)
-            kept = jnp.where((lane & 7) < ncs[0, l], kept, 0.0)
-            high = kept.astype(BF)
-            for part, value in enumerate([high, (kept - high.astype(F32)).astype(BF)]):
-                nr[part, j, :, 512 * l2 : 512 * l2 + 256] = value[0:16]
-                nr[part, j, :, 512 * l2 + 256 : 512 * l2 + 512] = value[16:32]
-        return 0
-
-    lax.fori_loop(0, 8, near_pair, 0)
-
     for o in range(1, 16):
         slot = lax.rem(own_client + o, 16)
         pltpu.make_async_copy(idxv.at[slot], idxv.at[slot], idx_rsem.at[slot]).wait()
     to_smem = pltpu.make_async_copy(idxv, idxs, load_sem.at[13])
     to_smem.start()
-    for i in (0, 1, 2, 3, 7, 5, 4, 6):
-        if i:
-            p1_copies[i].wait_recv()
-        wide = dot_nn(p1[i].reshape(128, 128), place_matrix(i % 4)).astype(BF)
-        for quad in range(8):
-            for a in range(4):
-                r2[32 * i + 4 * quad + a] = wide[
-                    16 * quad : 16 * quad + 16, 128 * a : 128 * a + 128
-                ]
+    for batch in (range(0, 4), range(4, 8)):
+        for i in batch:
+            if i:
+                p1_copies[i].wait_recv()
+        for i in batch:
+            wide = dot_nn(p1[i].reshape(128, 128), place_matrix(i % 4)).astype(BF)
+            for quad in range(8):
+                for a in range(4):
+                    r2[32 * i + 4 * quad + a] = wide[
+                        16 * quad : 16 * quad + 16, 128 * a : 128 * a + 128
+                    ]
     to_smem.wait()
     owners = []
     for i in range(8):
@@ -385,7 +379,17 @@
                 )
             )
 
-    lax.fori_loop(8, 16, near_pair, 0)
+    @pl.when(z >= 4)
+    def _():
+        inner_work()
+
+    for copy in halo_copies:
+        copy.wait_recv()
+    for j in range(2):
+        near_table(2 * j, halo[0, :, 128 * j : 128 * j + 128])
+        near_table(36 + 2 * j, halo[1, :, 128 * j : 128 * j + 128])
+    lax.fori_loop(0, 2, near_pair, 0)
+    lax.fori_loop(14, 16, near_pair, 0)
     row, col = iotas((1024, 128))
     group = row >> 8
     fold_near = ones_where(col == (group >> 1) * 64 + ((row & 255) >> 3) * 2 + (group & 1))
@@ -462,17 +466,16 @@
     dn[...] = dot_nn(dr[...].reshape(128, 512), ones_where(hit))
 
     loads["far_slots"].wait()
-    for o in range(16):
+    for o in range(1, 16):
         m = lax.rem(own_server + o, 16)
-        if o:
-            pltpu.make_async_copy(fbuf.at[m], fbuf.at[m], p2_rsem.at[m]).wait()
-        kind, at = lax.div(m, 8), lax.rem(m, 8)
-        wide = dot_nn(fbuf[m].reshape(32, 128), spread).astype(BF)
+        pltpu.make_async_copy(fbuf.at[m], fbuf.at[m], p2_rsem.at[m]).wait()
+    wide = dot_nn(fbuf[...].reshape(512, 128), spread).astype(BF)
+    for m in range(16):
         for i in range(8):
-            row_owner = lax.rem(z + i, 8) * 16 + at * 2
-            column_owner = at * 16 + lax.rem(y + i, 8) * 2 + 1
-            f = (1 - kind) * row_owner + kind * column_owner
-            row, lane = 16 * (i // 4), 128 * (i % 4)
+            row_owner = lax.rem(z + i, 8) * 16 + 2 * m
+            column_owner = (m - 8) * 16 + lax.rem(y + i, 8) * 2 + 1
+            f = row_owner if m < 8 else column_owner
+            row, lane = 32 * m + 16 * (i // 4), 128 * (i % 4)
             tt[f] = wide[row : row + 16, lane : lane + 128]
     _, col = iotas((16, 128))
     parts = [ones_where((col >> 5) == j) for j in range(4)]

time: 35.3 us -> 31.7 us (0.90)
  the two profiles are of different devices: /device:TPU:4 before, /device:TPU:1 now
where the time goes in v4:
time: 31.7 us; the launch traced here: 31.5 us
  Pallas kernels  30 us (95%)
  local copies, waits for them, and re-layouts  1.47 us (5%)
    pallas_call x1, Pallas kernels, per_device(): pl.pallas_call(kernel, out_shape=jax.ShapeDtypeStruct((16, 2048), BF), in...  30 us
    unnamed x1, local copies, waits for them, and re-layouts  1.47 us

profile of v4, /device:TPU:1, one launch (start us, length us, event | category | flops | bytes accessed | tf_op | source)
XLA Modules:
  0.0 31.5 jit_solution(15059206315062498093)
XLA Ops:
  0.0 30.0 %shard_map.127 = bf16[16,2048]{1,0:T(8,128)(2,1)} custom-call(bf16[16,2048]{1,0:T(8,128)(2,1)} %points_h.1, bf16[32,2048]{1,0:T(8,128)(2,1)} %basis_h.1, bf16[32,1024]{1,0:T(8,128)(2,1)} %transfer_h.1, bf16[32,16,1024]{2,1,0:T(8,128)(2,1)} %far_h.1, bf16[32,8,4096]{2,1,0:T(8,128)(2,1)} %near_h.1, s32[8,32]{1,0:T(8,128)} %bitcast.7, s32[1,32]{1,0:T(1,128)} %bitcast.8, ...), custom_call_target="tpu_custom_call" | custom-call | flops 60000000 | bytes 3600000 | tf_op jit(solution)/shard_map/pallas_call | solution.py:525
  30.0 1.5 %copy.15 = bf16[16,2048]{1,0:T(8,128)(2,1)} copy(bf16[16,2048]{1,0:T(8,128)(2,1)} %shard_map.127) | data formatting | bytes 131072

commit v5 on v4

--- a/solution.py
+++ b/solution.py
@@ -545,7 +545,7 @@
             vmem((128, 16, 128), BF),
             vmem((8, 512, 128), BF),
             vmem((8, 128, 256), BF),
-            vmem((512, 128), F32),
+            vmem((528, 128), F32),
             vmem((40, 32, 128), BF),
             vmem((2, 16, 16, 1024), BF),
             vmem((256, 128), F32),

time: 31.7 us -> 31.7 us (level)
  no operation moved by 1% of the time
where the time goes in v5:
time: 31.7 us; the launch traced here: 31.5 us
  Pallas kernels  30 us (95%)
  local copies, waits for them, and re-layouts  1.47 us (5%)
    pallas_call x1, Pallas kernels, per_device(): pl.pallas_call(kernel, out_shape=jax.ShapeDtypeStruct((16, 2048), BF), in...  30 us
    unnamed x1, local copies, waits for them, and re-layouts  1.47 us

profile of v5, /device:TPU:1, one launch (start us, length us, event | category | flops | bytes accessed | tf_op | source)
XLA Modules:
  0.0 31.5 jit_solution(17543355774155701162)
XLA Ops:
  0.0 30.0 %shard_map.127 = bf16[16,2048]{1,0:T(8,128)(2,1)} custom-call(bf16[16,2048]{1,0:T(8,128)(2,1)} %points_h.1, bf16[32,2048]{1,0:T(8,128)(2,1)} %basis_h.1, bf16[32,1024]{1,0:T(8,128)(2,1)} %transfer_h.1, bf16[32,16,1024]{2,1,0:T(8,128)(2,1)} %far_h.1, bf16[32,8,4096]{2,1,0:T(8,128)(2,1)} %near_h.1, s32[8,32]{1,0:T(8,128)} %bitcast.7, s32[1,32]{1,0:T(1,128)} %bitcast.8, ...), custom_call_target="tpu_custom_call" | custom-call | flops 60000000 | bytes 3600000 | tf_op jit(solution)/shard_map/pallas_call | solution.py:525
  30.0 1.5 %copy.15 = bf16[16,2048]{1,0:T(8,128)(2,1)} copy(bf16[16,2048]{1,0:T(8,128)(2,1)} %shard_map.127) | data formatting | bytes 131072
